TPU v7x, 128 devices: a whole 4x4x4 slice. The times are simulated.
128 devices in a mesh: branch: 16 (over z_hi, x, core), head: 8 (over z_lo, y).
Axes of the slice: x: 4, y: 4, z: 4 (z_hi: 2, z_lo: 2; z = z_hi * 2 + z_lo), core: 2. Of those that a mesh axis runs over, the one named last changes fastest.
Arguments:
- queries: bfloat16 [4, 16, 256, 8192], P(None, 'branch', None, 'head'), may hold values from -96 to 96
- key_rows: bfloat16 [4, 16, 256, 1024], P(None, 'branch', None, 'head'), may hold values from -4 to 4
- value_rows: bfloat16 [4, 16, 256, 1024], P(None, 'branch', None, 'head'), may hold values from -5 to 5
- cotangent: bfloat16 [4, 16, 256, 8192], P(None, 'branch', None, 'head'), may hold values from -6 to 6
- out_weight: bfloat16 [8192, 8192], P('head'), may hold values from -0.0625 to 0.0625
- parents: int32 [3, 16], replicated, may hold values from 0 to 15
- seg_len: int32 [4, 16], replicated, may hold values from 128 to 256, as said below
Outputs:
- query_grad: bfloat16 [4, 16, 256, 8192], P(None, 'branch', None, 'head')
- key_grad: bfloat16 [4, 16, 256, 1024], P(None, 'branch', None, 'head')
- value_grad: bfloat16 [4, 16, 256, 1024], P(None, 'branch', None, 'head')
Inputs may be any that keep to these rules, and one draw needn't show every extreme that they name: parents[m, j] is the node of level m that node j of level m + 1 continues; a node may have many children or none. `seg_len`: some node uses all 256 slots in every draw.
All inputs are finite; a program needn't handle non-finite values.
Results may differ from a plain program's by a relative error of at most 0.015.
Values may be sent and summed in bfloat16 or wider, within the bound.
No kernel may reach another device: no remote copies, remote signals or barrier semaphores. Data moves between devices by JAX's collectives and lax.ppermute only.
A program may use at most 192 MiB of HBM per device.

v0:
```python
import jax
import jax.numpy as jnp
from jax import lax
from jax.sharding import PartitionSpec as P

HD = 128


masked_score = -1e30


def pick_row(table, index_value):
    return lax.dynamic_index_in_dim(table, index_value, 0, keepdims=False)


def local(queries, key_rows, value_rows, cotangent, out_weight, parents, seg_len):
    levels, _, seg_rows, q_width = queries.shape
    kv_width = key_rows.shape[3]
    kv_local = kv_width // HD
    group_size = q_width // kv_width
    node_count = parents.shape[1]
    row_count = levels * seg_rows
    logit_scale = 1.0 / HD**0.5
    my_node = lax.axis_index("branch")
    piece = lax.all_gather(cotangent, "head", axis=3, tiled=True)
    piece_width = piece.shape[3]
    product = lax.dot_general(
        piece.reshape(row_count, piece_width),
        out_weight,
        (((1,), (1,)), ((), ())),
        preferred_element_type=jnp.float32,
    )
    dout_all = product
    dout_all = dout_all.astype(jnp.bfloat16).reshape(levels, seg_rows, q_width)
    key_all, value_all = (
        lax.all_gather(key_rows, "branch", axis=1, tiled=True),
        lax.all_gather(value_rows, "branch", axis=1, tiled=True),
    )
    positions = jnp.arange(seg_rows)
    grad_terms = jnp.zeros((levels, node_count, seg_rows, 2 * kv_width), jnp.float32)
    query_levels = [None] * levels
    for level_index in reversed(range(levels)):
        lineage = [None] * (level_index + 1)
        lineage[level_index] = my_node
        for ancestor_level in reversed(range(level_index)):
            lineage[ancestor_level] = pick_row(parents[ancestor_level], lineage[ancestor_level + 1])
        key_blocks = []
        value_blocks = []
        allowed_blocks = []
        for ancestor_level in range(level_index):
            key_blocks.append(pick_row(key_all[ancestor_level], lineage[ancestor_level]))
            value_blocks.append(pick_row(value_all[ancestor_level], lineage[ancestor_level]))
            length = pick_row(seg_len[ancestor_level], lineage[ancestor_level])
            allowed_blocks.append(
                jnp.broadcast_to(positions[None, :] < length, (seg_rows, seg_rows))
            )
        own_length = pick_row(seg_len[level_index], my_node)
        key_blocks.append(key_rows[level_index, 0])
        value_blocks.append(value_rows[level_index, 0])
        allowed_blocks.append(
            (positions[None, :] <= positions[:, None]) & (positions[None, :] < own_length)
        )
        key_cat = jnp.concatenate(key_blocks, axis=0)
        value_cat = jnp.concatenate(value_blocks, axis=0)
        allowed = jnp.concatenate(allowed_blocks, axis=1)
        key_count = key_cat.shape[0]
        key_heads = key_cat.reshape(key_count, kv_local, HD)
        value_heads = value_cat.reshape(key_count, kv_local, HD)
        query_heads = queries[level_index, 0].reshape(seg_rows, kv_local, group_size, HD)
        query_valid = positions < own_length
        dout_rows = jnp.where(
            query_valid[:, None], dout_all[level_index], jnp.zeros_like(dout_all[level_index])
        )
        dout_heads = dout_rows.reshape(seg_rows, kv_local, group_size, HD)
        score_matrix = (
            jnp.einsum("qngd,knd->ngqk", query_heads, key_heads, preferred_element_type=jnp.float32)
            * logit_scale
        )
        score_matrix = jnp.where(allowed[None, None], score_matrix, masked_score)
        maximum = jnp.max(score_matrix, axis=-1, keepdims=True)
        exponent = jnp.exp(score_matrix - maximum)
        softmax = exponent / jnp.sum(exponent, axis=-1, keepdims=True)
        probability_narrow = softmax.astype(jnp.bfloat16)
        attention_weights = jnp.einsum(
            "ngqk,knd->qngd", probability_narrow, value_heads, preferred_element_type=jnp.float32
        )
        delta_rows = jnp.sum(dout_heads.astype(jnp.float32) * attention_weights, axis=-1)
        probability_gradient = jnp.einsum(
            "qngd,knd->ngqk", dout_heads, value_heads, preferred_element_type=jnp.float32
        )
        dscores = softmax * (probability_gradient - jnp.transpose(delta_rows, (1, 2, 0))[..., None])
        score_gradient_narrow = dscores.astype(jnp.bfloat16)
        query_portion = (
            jnp.einsum(
                "ngqk,knd->qngd",
                score_gradient_narrow,
                key_heads,
                preferred_element_type=jnp.float32,
            )
            * logit_scale
        )
        query_levels[level_index] = query_portion.astype(jnp.bfloat16).reshape(1, seg_rows, q_width)
        key_portion = (
            jnp.einsum(
                "ngqk,qngd->knd",
                score_gradient_narrow,
                query_heads,
                preferred_element_type=jnp.float32,
            )
            * logit_scale
        )
        value_portion = jnp.einsum(
            "ngqk,qngd->knd", probability_narrow, dout_heads, preferred_element_type=jnp.float32
        )
        key_value_grad = jnp.concatenate(
            [key_portion.reshape(key_count, kv_width), value_portion.reshape(key_count, kv_width)],
            axis=1,
        )
        for ancestor_level in range(level_index + 1):
            block = key_value_grad[ancestor_level * seg_rows : (ancestor_level + 1) * seg_rows]
            corner = (
                jnp.int32(ancestor_level),
                lineage[ancestor_level],
                jnp.int32(0),
                jnp.int32(0),
            )
            current = lax.dynamic_slice(grad_terms, corner, (1, 1, seg_rows, 2 * kv_width))
            grad_terms = lax.dynamic_update_slice(grad_terms, current + block[None, None], corner)
    summed = lax.psum_scatter(grad_terms, "branch", scatter_dimension=1, tiled=True)
    query_grad = jnp.stack(query_levels, axis=0)
    key_grad = summed[..., :kv_width].astype(jnp.bfloat16)
    value_grad = summed[..., kv_width:].astype(jnp.bfloat16)
    return (query_grad, key_grad, value_grad)


def solution(mesh):
    in_specs = (
        P(None, "branch", None, "head"),
        P(None, "branch", None, "head"),
        P(None, "branch", None, "head"),
        P(None, "branch", None, "head"),
        P("head", None),
        P(),
        P(),
    )
    out_specs = (
        P(None, "branch", None, "head"),
        P(None, "branch", None, "head"),
        P(None, "branch", None, "head"),
    )
    return jax.shard_map(local, mesh=mesh, in_specs=in_specs, out_specs=out_specs, check_vma=False)
```

profile of v0, /device:TPU:0, one launch (start us, length us, event | category | flops | bytes accessed | tf_op | source)
XLA Modules:
  0.0 593.7 jit_solution(2356493267750828133)
XLA Ops:
  21.7 1.8 fusion.186
  23.7 1.0 copy.180
  36.3 1.3 fusion.190
  38.6 1.6 slice_bitcast_fusion.5
  40.2 1.6 slice_bitcast_fusion.4
  42.7 1.3 fusion.99
  44.0 25.0 %all-gather.8.cloned.1.call-done = bf16[4,16,256,128]{3,2,1,0:T(8,128)(2,1)} async-done(((bf16[4,1,256,128]{3,2,1,0:T(8,128)(2,1)}), bf16[4,16,256,128]{3,2,1,0:T(8,128)(2,1)}) %all-gather.8.cloned.1.call-update) | async-done | bytes 4194320 | tf_op jit(solution)/shard_map/all_gather | solution.py:37
  69.1 3.5 fusion.184
  73.2 53.0 %all-gather.6.cloned.1.call-done = bf16[4,16,256,128]{3,2,1,0:T(8,128)(2,1)} async-done(((bf16[4,1,256,128]{3,2,1,0:T(8,128)(2,1)}), bf16[4,16,256,128]{3,2,1,0:T(8,128)(2,1)}) %all-gather.6.cloned.1.call-update) | async-done | bytes 4194320 | tf_op jit(solution)/shard_map/all_gather | solution.py:36
  126.3 2.2 fusion.183
  128.5 1.6 dynamic-slice_bitcast_fusion.6
  130.1 1.6 dynamic-slice_bitcast_fusion.10
  132.6 1.9 fusion.19
  134.5 1.1 fusion.9
  135.7 1.4 fusion.4
  137.1 2.6 fusion.8
  139.7 1.1 copy-done.3
  140.8 2.3 fusion.3
  143.1 154.0 %all-gather.4.cloned.1.call-done = bf16[4,1,256,8192]{3,2,1,0:T(8,128)(2,1)} async-done(((bf16[4,1,256,1024]{3,2,1,0:T(8,128)(2,1)}), bf16[4,1,256,8192]{3,2,1,0:T(8,128)(2,1)}) %all-gather.4.cloned.1.call-update) | async-done | bytes 16777232 | tf_op jit(solution)/shard_map/all_gather | solution.py:25
  297.2 22.2 %convolution_convert_fusion = bf16[1024,1024]{0,1:T(8,128)(2,1)S(1)} fusion(bf16[1024,8192]{1,0:T(8,128)(2,1)} %bitcast.525, bf16[1024,8192]{1,0:T(8,128)(2,1)} %param.11), kind=kOutput, calls=%fused_computation.51 | convolution fusion | flops 17180917760 | bytes 35651584 | tf_op jit(solution)/shard_map/dot_general | solution.py:27
  321.7 1.1 fusion.96
  322.8 1.2 fusion.68
  324.1 1.3 fusion.72
  325.5 1.5 fusion.12
  328.4 1.9 fusion.76
  330.4 3.4 fusion.21
  333.8 1.1 fusion.86
  335.0 1.4 fusion.67
  336.5 2.4 fusion.69
  339.0 4.5 fusion.10
  343.5 1.5 fusion.82
  345.8 1.1 convolution_bitcast_fusion.3
  347.9 4.4 fusion.87
  353.4 4.9 fusion.83
  358.6 5.1 fusion.79
  364.7 7.9 %broadcast_in_dim.210 = f32[4,16,256,256]{2,3,1,0:T(8,128)} broadcast(f32[]{:T(128)} %constant.118.clone.1), dimensions={} | broadcast | bytes 16777220 | tf_op jit(solution)/shard_map/broadcast_in_dim | solution.py:40
  373.2 1.7 fusion.130
  374.9 1.7 fusion.123
  376.6 1.7 fusion.139
  378.3 1.7 fusion.119
  380.0 1.7 fusion.115
  381.7 1.7 fusion.136
  383.4 1.7 fusion.111
  385.1 1.7 fusion.133
  386.8 1.7 fusion.141
  388.5 193.2 %all-reduce.2 = bf16[4,16,256,256]{2,3,1,0:T(8,128)(2,1)} all-reduce(f32[4,16,256,256]{2,3,1,0:T(8,128)} %fusion.141), channel_id=2, replica_groups=mesh['branch'=16,'head'=8] {'branch'}, use_global_device_ids=true, to_apply=%region_12.13.clone | all-reduce | flops 4194304 | bytes 25165824
  581.7 1.7 dynamic-slice_convert_fusion
  585.1 1.6 pad_maximum_fusion
  (210 shorter events, 27.8 us)
Async XLA Ops:
  7.2 18.8 %copy-start.72 = (u32[128]{0:T(128)S(1)}, u32[128]{0:T(128)}, u32[]{:S(2)}) copy-start(u32[128]{0:T(128)} %constant.129) | copy-start | bytes 1540
  7.2 21.3 %copy-start.71 = (s32[4,16]{1,0:T(4,128)S(1)}, s32[4,16]{1,0:T(4,128)}, u32[]{:S(2)}) copy-start(s32[4,16]{1,0:T(4,128)} %param.13) | copy-start | bytes 772
  7.2 61.9 %all-gather.8.cloned.1.call-start = ((), (), s32[]{:S(2)}) async-start(), calls=%async_computation.2 | async-start | bytes 4456448 | tf_op jit(solution)/shard_map/all_gather | solution.py:37
  7.9 118.3 %all-gather.6.cloned.1.call-start = ((), (), s32[]{:S(2)}) async-start(), calls=%async_computation.1 | async-start | bytes 4456448 | tf_op jit(solution)/shard_map/all_gather | solution.py:36
  8.7 288.5 %all-gather.4.cloned.1.call-start = ((), (), s32[]{:S(2)}) async-start(), calls=%async_computation | async-start | bytes 18874368 | tf_op jit(solution)/shard_map/all_gather | solution.py:25
  31.0 7.4 %copy-start.63 = (pred[256]{0:T(512)(128)(4,1)}, pred[256]{0:T(512)(128)(4,1)S(1)}, u32[]{:S(2)}) copy-start(pred[256]{0:T(512)(128)(4,1)S(1)} %iota_compare_fusion.5) | copy-start | bytes 772
  31.6 6.8 %copy-start.60 = (pred[256]{0:T(512)(128)(4,1)}, pred[256]{0:T(512)(128)(4,1)S(1)}, u32[]{:S(2)}) copy-start(pred[256]{0:T(512)(128)(4,1)S(1)} %iota_compare_fusion.1) | copy-start | bytes 772
  32.8 5.6 copy-start.66
  33.5 4.1 copy-start.69
  38.0 4.7 copy-start.47
  126.3 5.5 copy-start.19
  128.5 6.0 %copy-start.4 = (bf16[1,1,256,1024]{2,3,1,0:T(8,128)(2,1)S(1)}, bf16[1,1,256,1024]{2,3,1,0:T(8,128)(2,1)}, u32[]{:S(2)}) copy-start(bf16[1,1,256,1024]{2,3,1,0:T(8,128)(2,1)} %copy.180) | copy-start | bytes 1572868
  128.5 7.1 %copy-start.29 = (bf16[256,128]{1,0:T(8,128)(2,1)}, bf16[256,128]{1,0:T(8,128)(2,1)S(1)}, u32[]{:S(2)}) copy-start(bf16[256,128]{1,0:T(8,128)(2,1)S(1)} %dynamic-slice_bitcast_fusion.3) | copy-start | bytes 196612
  130.1 5.5 copy-start.15
  130.1 5.5 copy-start.33
  131.7 3.8 copy-start.17
  131.7 3.8 copy-start.21
  131.8 3.9 copy-start.35
  132.5 4.5 copy-start.1
  135.6 4.1 copy-start
  135.6 4.1 copy-start.49
  297.2 22.2 %copy-start.61 = (pred[256]{0:T(512)(128)(4,1)S(1)}, pred[256]{0:T(512)(128)(4,1)}, u32[]{:S(2)}) copy-start(pred[256]{0:T(512)(128)(4,1)} %copy-done.60) | copy-start | bytes 772
  297.2 22.3 %copy-start.64 = (pred[256]{0:T(512)(128)(4,1)S(1)}, pred[256]{0:T(512)(128)(4,1)}, u32[]{:S(2)}) copy-start(pred[256]{0:T(512)(128)(4,1)} %copy-done.63) | copy-start | bytes 772
  297.2 22.3 %copy-start.67 = (pred[256]{0:T(512)(128)(4,1)S(1)}, pred[256]{0:T(512)(128)(4,1)}, u32[]{:S(2)}) copy-start(pred[256]{0:T(512)(128)(4,1)} %copy-done.66) | copy-start | bytes 772
  297.2 22.3 %copy-start.70 = (pred[256]{0:T(512)(128)(4,1)S(1)}, pred[256]{0:T(512)(128)(4,1)}, u32[]{:S(2)}) copy-start(pred[256]{0:T(512)(128)(4,1)} %copy-done.69) | copy-start | bytes 772
  319.8 4.2 copy-start.25
  319.9 8.5 %copy-start.24 = (bf16[256,1024]{0,1:T(8,128)(2,1)}, bf16[256,1024]{0,1:T(8,128)(2,1)S(1)}, u32[]{:S(2)}) copy-start(bf16[256,1024]{0,1:T(8,128)(2,1)S(1)} %get-tuple-element.24) | copy-start | bytes 1572868
  319.9 16.6 %copy-start.23 = (bf16[256,1024]{0,1:T(8,128)(2,1)}, bf16[256,1024]{0,1:T(8,128)(2,1)S(1)}, u32[]{:S(2)}) copy-start(bf16[256,1024]{0,1:T(8,128)(2,1)S(1)} %get-tuple-element.23) | copy-start | bytes 1572868
  324.1 4.3 slice-start
  328.4 8.0 %slice-start.2 = ((s8[8388608]{0:T(1024)(128)(4,1)}), s8[4194304]{0:T(1024)(128)(4,1)S(1)}, s32[]{:S(2)}) async-start(s8[8388608]{0:T(1024)(128)(4,1)} %bitcast.499), calls=%async_computation.5 | async-start | bytes 8388608
  330.3 4.7 copy-start.16
  330.3 4.7 copy-start.18
  330.4 6.1 %slice-start.3 = ((s8[8388608]{0:T(1024)(128)(4,1)}), s8[4194304]{0:T(1024)(128)(4,1)S(1)}, s32[]{:S(2)}) async-start(s8[8388608]{0:T(1024)(128)(4,1)} %bitcast.499), calls=%async_computation.6 | async-start | bytes 8388608
  339.0 4.5 copy-start.27
  343.5 4.4 copy-start.52
  343.5 4.4 copy-start.68
  347.9 5.4 copy-start.54
  347.9 5.4 copy-start.65
  353.4 5.0 copy-start.9
  353.4 5.2 copy-start.57
  353.4 5.2 copy-start.59
  353.4 5.2 copy-start.62
  372.5 10.9 %copy-start.13 = (f32[512,128]{0,1:T(8,128)S(1)}, f32[512,128]{0,1:T(8,128)}, u32[]{:S(2)}) copy-start(f32[512,128]{0,1:T(8,128)} %fusion.87) | copy-start | bytes 786436
  372.5 14.3 %copy-start.28 = (f32[256,128]{0,1:T(8,128)S(1)}, f32[256,128]{0,1:T(8,128)}, u32[]{:S(2)}) copy-start(f32[256,128]{0,1:T(8,128)} %fusion.96) | copy-start | bytes 393220
  372.5 14.3 %copy-start.37 = (f32[256,128]{0,1:T(8,128)S(1)}, f32[256,128]{0,1:T(8,128)}, u32[]{:S(2)}) copy-start(f32[256,128]{0,1:T(8,128)} %convolution_bitcast_fusion.3) | copy-start | bytes 393220
  388.5 196.6 %copy-start.6 = (bf16[1,1,256,1024]{3,2,1,0:T(8,128)(2,1)S(1)}, bf16[1,1,256,1024]{3,2,1,0:T(8,128)(2,1)}, u32[]{:S(2)}) copy-start(bf16[1,1,256,1024]{3,2,1,0:T(8,128)(2,1)} %copy.121) | copy-start | bytes 1572868
  388.5 196.6 %copy-start.7 = (bf16[1,1,256,1024]{3,2,1,0:T(8,128)(2,1)S(1)}, bf16[1,1,256,1024]{3,2,1,0:T(8,128)(2,1)}, u32[]{:S(2)}) copy-start(bf16[1,1,256,1024]{3,2,1,0:T(8,128)(2,1)} %copy.122) | copy-start | bytes 1572868
  388.5 196.6 %copy-start.8 = (bf16[1,1,256,1024]{3,2,1,0:T(8,128)(2,1)S(1)}, bf16[1,1,256,1024]{3,2,1,0:T(8,128)(2,1)}, u32[]{:S(2)}) copy-start(bf16[1,1,256,1024]{3,2,1,0:T(8,128)(2,1)} %copy.124) | copy-start | bytes 1572868
  (32 other events, 83.0 us)
Sparse Core Ops, SparseCore 0:
  10.5 58.5 all-gather.7
  71.5 54.6 all-gather.5
  127.9 169.2 all-gather.3
where the time goes:
time: 603 us; the launch traced here: 594 us
  waiting for transfers between devices  234 us (39%)
  blocking collectives  193 us (32%)
  matrix products  66.6 us (11%)
  local copies, waits for them, and re-layouts  38.2 us (6%)
  other arithmetic  34.2 us (6%)
  between operations  27.1 us (4%)
    unnamed x1, blocking collectives  193 us
    all_gather x1, waiting for transfers between devices, local(): piece = lax.all_gather(cotangent, 'head', axis=3, tiled=True)  154 us
    all_gather x1, waiting for transfers between devices, local(): lax.all_gather(key_rows, 'branch', axis=1, tiled=True)  53 us
    all_gather x1, waiting for transfers between devices, local(): lax.all_gather(value_rows, 'branch', axis=1, tiled=True)  25 us
    dot_general x1, matrix products, local(): lax.dot_general(piece.reshape(row_count, piece_width), out_weight, (((1,)...  22.2 us
    dynamic_update_slice x10, other arithmetic, local(): lax.dynamic_update_slice(grad_terms, current + block[None, None], corner)  16 us
    dot_general x4, matrix products, local(): jnp.einsum('ngqk,qngd->knd', probability_narrow, dout_heads, preferred_el...  15.5 us
  transfers between devices with their start and end apart: 3, of which 3 were waited for; matrix products, arithmetic and copies ran while one was open for 7% of the time, Pallas kernels for 0%

commit v1 on v0

v1 whole, which is shorter than its diff:
```python
import functools

import jax
import jax.numpy as jnp
from jax import lax
from jax.experimental import pallas as pl
from jax.experimental.pallas import tpu as pltpu
from jax.sharding import Mesh, PartitionSpec as P

HD = 128
SEG = 256
GROUP = 8
LEVELS = 4
NODES = 16
FEATURES = 1024
HALF = 4096
PIECE = 128
SCALE = 1.0 / HD**0.5
MASKED = -1e30
NT = (((1,), (1,)), ((), ()))
AXES = ("zh", "x", "c")
ALT = [(0, 3), (1, 2), (2, 1), (3, 0)]
SWAP = [(0, 1), (1, 0)]
UP = [(i, (i + 1) % 4) for i in range(4)]
DOWN = [(i, (i + 3) % 4) for i in range(4)]


def cost(flops, size, exps=0):
    return pl.CostEstimate(flops=flops, bytes_accessed=size, transcendentals=exps)


def node_id(meta):
    return (meta[0] * 4 + meta[1]) * 2 + meta[2]


def ancestor(parents, node, level, target):
    for m in reversed(range(target, level)):
        node = parents[m * NODES + node]
    return node


def relative(meta, node):
    zh = lax.rem(node // 8 + meta[0], 2)
    x = lax.rem(lax.rem(node // 2, 4) - meta[1] + 4, 4)
    c = lax.rem(lax.rem(node, 2) + meta[2], 2)
    return (c * 4 + x) * 2 + zh


def own_product_kernel(meta, cot, weight, out):
    step = pl.program_id(1)
    part = lax.dot_general(cot[0], weight[...], NT, preferred_element_type=jnp.float32)

    @pl.when(step == 0)
    def _():
        out[...] = part

    @pl.when(step > 0)
    def _():
        out[...] += part


def own_product(meta, cot, weight):
    width = weight.shape[0]
    columns = 512
    return pl.pallas_call(
        own_product_kernel,
        grid_spec=pltpu.PrefetchScalarGridSpec(
            num_scalar_prefetch=1,
            grid=(width // columns, 4),
            in_specs=[
                pl.BlockSpec((1, SEG, FEATURES), lambda n, k, meta: (k, 0, 0)),
                pl.BlockSpec((columns, FEATURES), lambda n, k, meta: (n, meta[3] * 4 + k)),
            ],
            out_specs=pl.BlockSpec((SEG, columns), lambda n, k, meta: (0, n)),
        ),
        out_shape=jax.ShapeDtypeStruct((SEG, width), jnp.float32),
        compiler_params=pltpu.CompilerParams(vmem_limit_bytes=32 * 2**20),
        cost_estimate=cost(2 * SEG * width * HALF, 2 * width * HALF + 6 * SEG * width),
        name="own_product",
    )(meta, cot, weight)


def partner_product_kernel(cot, *refs):
    pieces, out, total = refs[:8], refs[8], refs[9]
    step = pl.program_id(0)
    rows = jnp.concatenate([piece[...] for piece in pieces], axis=0)
    part = lax.dot_general(cot[0], rows, NT, preferred_element_type=jnp.float32)

    @pl.when(step == 0)
    def _():
        total[...] = part

    @pl.when(step > 0)
    def _():
        total[...] += part

    @pl.when(step == 3)
    def _():
        for p in range(8):
            out[p] = total[:, p * PIECE : (p + 1) * PIECE].astype(jnp.bfloat16)


def partner_product(cot, pieces):
    return pl.pallas_call(
        partner_product_kernel,
        grid=(4,),
        in_specs=[pl.BlockSpec((1, SEG, FEATURES), lambda k: (k, 0, 0))]
        + [pl.BlockSpec((PIECE, FEATURES), lambda k: (0, k))] * 8,
        out_specs=pl.BlockSpec((8, SEG, PIECE), lambda k: (0, 0, 0)),
        out_shape=jax.ShapeDtypeStruct((8, SEG, PIECE), jnp.bfloat16),
        scratch_shapes=[pltpu.VMEM((SEG, 8 * PIECE), jnp.float32)],
        compiler_params=pltpu.CompilerParams(vmem_limit_bytes=32 * 2**20),
        cost_estimate=cost(2 * SEG * 1024 * HALF, 2 * 1024 * HALF + 4 * SEG * 1024),
        name="partner_product",
    )(cot, *pieces)


def probs_kernel(level, meta, parents, lengths, query, own_key, *refs):
    keys, out = refs[:level], refs[level]
    me = node_id(meta)
    q = query[0, 0]
    blocks = []
    for m in range(level + 1):
        key = keys[m][0, 0, 0] if m < level else own_key[0, 0]
        s = lax.dot_general(key, q, NT, preferred_element_type=jnp.float32)
        length = lengths[m * NODES + ancestor(parents, me, level, m)]
        position = lax.broadcasted_iota(jnp.int32, (SEG, SEG), 0)
        allowed = position < length
        if m == level:
            allowed = allowed & (position <= lax.broadcasted_iota(jnp.int32, (SEG, SEG), 1))
        blocks.append(jnp.where(allowed, s, MASKED))
    top = functools.reduce(jnp.maximum, [jnp.max(s, axis=0, keepdims=True) for s in blocks])
    exps = [jnp.exp((s - top) * SCALE) for s in blocks]
    inverse = 1.0 / sum(jnp.sum(e, axis=0, keepdims=True) for e in exps)
    for m in range(level + 1):
        out[0, m * SEG : (m + 1) * SEG] = (exps[m] * inverse).astype(jnp.bfloat16)


def gathered_spec(level, target, part):
    def index(h, meta, parents, lengths):
        node = ancestor(parents, node_id(meta), level, target)
        return relative(meta, node), target, part, 0, 0

    return pl.BlockSpec((1, 1, 1, SEG, HD), index)


def probs(level, meta, parents, lengths, queries, key_rows, gathered):
    count = (level + 1) * SEG
    return pl.pallas_call(
        functools.partial(probs_kernel, level),
        grid_spec=pltpu.PrefetchScalarGridSpec(
            num_scalar_prefetch=3,
            grid=(GROUP,),
            in_specs=[
                pl.BlockSpec((1, 1, SEG, HD), lambda h, *_: (level, 0, 0, h)),
                pl.BlockSpec((1, 1, SEG, HD), lambda h, *_: (level, 0, 0, 0)),
            ]
            + [gathered_spec(level, m, 0) for m in range(level)],
            out_specs=pl.BlockSpec((1, count, SEG), lambda h, *_: (h, 0, 0)),
        ),
        out_shape=jax.ShapeDtypeStruct((GROUP, count, SEG), jnp.bfloat16),
        compiler_params=pltpu.CompilerParams(vmem_limit_bytes=32 * 2**20),
        cost_estimate=cost(
            2 * GROUP * count * SEG * HD, 2 * GROUP * count * SEG, GROUP * count * SEG
        ),
        name=f"probs_{level}",
    )(meta, parents, lengths, queries, key_rows, *[gathered] * level)


def backward_kernel(
    level, meta, parents, lengths, probs_ref, query, own, partner, own_key, own_value, *refs
):
    keys, refs = refs[:level], refs[level:]
    values, refs = refs[:level], refs[level:]
    if level:
        query_out, own_out, ancestor_out, flipped, key_total, value_total = refs
    else:
        query_out, own_out, flipped, key_total, value_total = refs
    head = pl.program_id(0)
    blocks = [slice(m * SEG, (m + 1) * SEG) for m in range(level + 1)]
    key_blocks = [keys[m][0, 0, 0] for m in range(level)] + [own_key[0, 0]]
    value_blocks = [values[m][0, 0, 0] for m in range(level)] + [own_value[0, 0]]

    @pl.when(head == 0)
    def _():
        key_total[...] = jnp.zeros_like(key_total)
        value_total[...] = jnp.zeros_like(value_total)
        for m in range(level + 1):
            flipped[:, blocks[m]] = key_blocks[m].astype(jnp.float32).T.astype(jnp.bfloat16)

    length = lengths[level * NODES + node_id(meta)]
    position = lax.broadcasted_iota(jnp.int32, (SEG, HD), 0)
    total = own[...] + partner[0].astype(jnp.float32)
    dout = jnp.where(position < length, total, 0.0).astype(jnp.bfloat16)
    q = query[0, 0]
    wide = [probs_ref[0, block].astype(jnp.float32) for block in blocks]
    grads = [
        lax.dot_general(value, dout, NT, preferred_element_type=jnp.float32)
        for value in value_blocks
    ]
    delta = sum(jnp.sum(p * g, axis=0, keepdims=True) for p, g in zip(wide, grads))
    query_total = jnp.zeros((HD, SEG), jnp.float32)
    for m in range(level + 1):
        scores = (wide[m] * (grads[m] - delta)).astype(jnp.bfloat16)
        key_total[blocks[m]] += jnp.dot(scores, q, preferred_element_type=jnp.float32)
        value_total[blocks[m]] += jnp.dot(
            probs_ref[0, blocks[m]], dout, preferred_element_type=jnp.float32
        )
        query_total += jnp.dot(
            flipped[:, blocks[m]], scores, preferred_element_type=jnp.float32
        )
    query_out[...] = (query_total * SCALE).T.astype(jnp.bfloat16)

    @pl.when(head == GROUP - 1)
    def _():
        for m in range(level):
            ancestor_out[m, 0] = (key_total[blocks[m]] * SCALE).astype(jnp.bfloat16)
            ancestor_out[m, 1] = value_total[blocks[m]].astype(jnp.bfloat16)
        own_out[0] = key_total[blocks[level]] * SCALE
        own_out[1] = value_total[blocks[level]]


def backward(
    level, meta, parents, lengths, probabilities, queries, own, partner, key_rows, value_rows, gathered
):
    count = (level + 1) * SEG
    width = GROUP * HD

    def piece_index(h, meta, *_):
        quarter = lax.rem(h // 2 - meta[1] + 4, 4)
        return lax.rem(lax.rem(h, 2) + meta[2], 2) * 4 + quarter, 0, 0

    out_specs = [
        pl.BlockSpec((SEG, HD), lambda h, *_: (0, h)),
        pl.BlockSpec((2, SEG, HD), lambda h, *_: (0, 0, 0)),
    ]
    out_shape = [
        jax.ShapeDtypeStruct((SEG, width), jnp.bfloat16),
        jax.ShapeDtypeStruct((2, SEG, HD), jnp.float32),
    ]
    if level:
        out_specs.append(pl.BlockSpec((level, 2, SEG, HD), lambda h, *_: (0, 0, 0, 0)))
        out_shape.append(jax.ShapeDtypeStruct((level, 2, SEG, HD), jnp.bfloat16))
    return pl.pallas_call(
        functools.partial(backward_kernel, level),
        grid_spec=pltpu.PrefetchScalarGridSpec(
            num_scalar_prefetch=3,
            grid=(GROUP,),
            in_specs=[
                pl.BlockSpec((1, count, SEG), lambda h, *_: (h, 0, 0)),
                pl.BlockSpec((1, 1, SEG, HD), lambda h, *_: (level, 0, 0, h)),
                pl.BlockSpec((SEG, HD), lambda h, *_: (0, h)),
                pl.BlockSpec((1, SEG, PIECE), piece_index),
                pl.BlockSpec((1, 1, SEG, HD), lambda h, *_: (level, 0, 0, 0)),
                pl.BlockSpec((1, 1, SEG, HD), lambda h, *_: (level, 0, 0, 0)),
            ]
            + [gathered_spec(level, m, 0) for m in range(level)]
            + [gathered_spec(level, m, 1) for m in range(level)],
            out_specs=out_specs,
            scratch_shapes=[
                pltpu.VMEM((HD, count), jnp.bfloat16),
                pltpu.VMEM((count, HD), jnp.float32),
                pltpu.VMEM((count, HD), jnp.float32),
            ],
        ),
        out_shape=out_shape,
        compiler_params=pltpu.CompilerParams(vmem_limit_bytes=32 * 2**20),
        cost_estimate=cost(8 * GROUP * count * SEG * HD, 2 * GROUP * count * SEG),
        name=f"backward_{level}",
    )(
        meta, parents, lengths, probabilities, queries, own, partner, key_rows, value_rows,
        *[gathered] * (2 * level),
    )


def spread_kernel(target, meta, parents, *refs):
    terms, out = refs[:-1], refs[-1]
    slot = pl.program_id(0)
    me = node_id(meta)
    sibling = me + 1 - 2 * meta[2]
    wanted = (lax.rem(slot, 2) * 4 + slot // 2) * 2 + meta[2]
    total = jnp.zeros(out.shape[1:], jnp.float32)
    count = LEVELS - 1 - target
    for i, term in enumerate(terms):
        level = target + 1 + i % count
        node = me if i < count else sibling
        hit = ancestor(parents, node, level, target) == wanted
        total += jnp.where(hit, term[0].astype(jnp.float32), 0.0)
    out[0] = total.astype(jnp.bfloat16)


def spread(target, meta, parents, terms):
    return pl.pallas_call(
        functools.partial(spread_kernel, target),
        grid_spec=pltpu.PrefetchScalarGridSpec(
            num_scalar_prefetch=2,
            grid=(8,),
            in_specs=[pl.BlockSpec((1, 2, SEG, HD), lambda n, *_: (target, 0, 0, 0))] * len(terms),
            out_specs=pl.BlockSpec((1, 2, SEG, HD), lambda n, *_: (n, 0, 0, 0)),
        ),
        out_shape=jax.ShapeDtypeStruct((8, 2, SEG, HD), jnp.bfloat16),
        compiler_params=pltpu.CompilerParams(vmem_limit_bytes=32 * 2**20),
        cost_estimate=cost(8 * len(terms) * 2 * SEG * HD, 16 * 2 * SEG * HD),
        name=f"spread_{target}",
    )(meta, parents, *terms)


def gather_rows(key_rows, value_rows):
    own = jnp.stack([key_rows[: LEVELS - 1, 0], value_rows[: LEVELS - 1, 0]], axis=1)
    pair = jnp.stack([own, lax.ppermute(own, "zh", SWAP)])
    below = lax.ppermute(pair, "x", UP)
    above = lax.ppermute(pair, "x", DOWN)
    across = jnp.stack(
        [lax.ppermute(above[0], "x", DOWN), lax.ppermute(below[1], "x", UP)]
    )
    mine = jnp.concatenate([pair, above, across, below])
    return jnp.concatenate([mine, lax.ppermute(mine, "c", SWAP)])


def partner_weight(out_weight, zh, x, c, zl):
    def rows(quarter):
        return lax.dynamic_slice(
            out_weight, (quarter * 256 + c * PIECE, (1 - zl) * HALF), (PIECE, HALF)
        )

    first = lax.ppermute(rows(x), "zl", SWAP)
    second = lax.ppermute(rows(lax.rem(x + 1, 4)), ("zh", "zl"), ALT)
    third = lax.ppermute(second, "x", DOWN)
    fourth = lax.ppermute(first, "x", UP)
    mine = [first, second, third, fourth]
    return mine + [lax.ppermute(piece, "c", SWAP) for piece in mine]


def local(queries, key_rows, value_rows, cotangent, out_weight, parents, seg_len):
    zh, x, c, zl, y = [lax.axis_index(name) for name in ("zh", "x", "c", "zl", "y")]
    meta = jnp.stack([zh, x, c, zl, y]).astype(jnp.int32)
    parents = parents.reshape(-1)
    lengths = seg_len.reshape(-1)
    cots = [None] * LEVELS
    for level in reversed(range(LEVELS)):
        cots[level] = lax.all_gather(cotangent[level, 0], "y")
    weights = partner_weight(out_weight, zh, x, c, zl)
    gathered = gather_rows(key_rows, value_rows)
    query_grads = [None] * LEVELS
    own_grads = [None] * LEVELS
    terms = [None] * LEVELS
    passed = [None] * LEVELS
    sums = [None] * LEVELS
    for level in reversed(range(LEVELS)):
        partner = lax.ppermute(partner_product(cots[level], weights), "zl", SWAP)
        own = own_product(meta, cots[level], out_weight)
        probabilities = probs(level, meta, parents, lengths, queries, key_rows, gathered)
        results = backward(
            level, meta, parents, lengths, probabilities, queries, own, partner,
            key_rows, value_rows, gathered,
        )
        query_grads[level], own_grads[level] = results[:2]
        if level:
            terms[level] = results[2]
            passed[level] = lax.ppermute(results[2], "c", SWAP)
            target = level - 1
            dense = spread(target, meta, parents, terms[level:] + passed[level:])
            part = lax.psum_scatter(
                dense.reshape(4, 2, 2, SEG, HD), "x", scatter_dimension=0, tiled=False
            )
            kept = lax.dynamic_index_in_dim(part, zh, 0, keepdims=False)
            given = lax.dynamic_index_in_dim(part, 1 - zh, 0, keepdims=False)
            sums[target] = (kept, lax.ppermute(given, "zh", SWAP))
    finals = [
        (own_grads[t] + sums[t][0].astype(jnp.float32) + sums[t][1].astype(jnp.float32))
        for t in range(LEVELS - 1)
    ] + [own_grads[LEVELS - 1]]
    query_grad = jnp.stack(query_grads)[:, None]
    key_grad = jnp.stack([f[0] for f in finals])[:, None].astype(jnp.bfloat16)
    value_grad = jnp.stack([f[1] for f in finals])[:, None].astype(jnp.bfloat16)
    return (query_grad, key_grad, value_grad)


def solution(mesh):
    fine = Mesh(mesh.devices.reshape(2, 4, 2, 2, 4), ("zh", "x", "c", "zl", "y"))
    rows = P(None, AXES, None, ("zl", "y"))
    in_specs = (rows, rows, rows, rows, P(("zl", "y"), None), P(), P())
    return jax.shard_map(
        local, mesh=fine, in_specs=in_specs, out_specs=(rows, rows, rows), check_vma=False
    )
```

time: 603 us -> 308 us (0.51); the launches traced: 594 us -> 306 us
  blocking collectives: 193 us -> 0 us
  waiting for transfers between devices: 234 us -> 59 us
  Pallas kernels: 0 us -> 113 us
  matrix products: 66.6 us -> 0 us
  local copies, waits for them, and re-layouts: 38.2 us -> 83.6 us
  starting transfers between devices: 0.11 us -> 28.7 us
  other arithmetic: 34.2 us -> 6.56 us
  between operations: 27.1 us -> 15 us
    all_gather x3 -> x4, waiting for transfers between devices: 232 us -> 0.06 us  [local(): cots[level] = lax.all_gather(cotangent[level, 0], 'y')]
    unnamed x1 -> x0, blocking collectives: 193 us -> none
    pallas_call x0 -> x19, Pallas kernels: none -> 113 us  [the longest x4 42.1 us: backward(): pl.pallas_call(functools.partial(backward_kernel, level), grid_spec=pltpu...]
    dot_general x25 -> x0, matrix products: 66.6 us -> none  [the longest x1 22.2 us: local(): lax.dot_general(piece.reshape(row_count, piece_width), out_weight, (((1,)...]
    unnamed x161 -> x154, local copies, waits for them, and re-layouts: 7.01 us -> 70.1 us
    ppermute x0 -> x24, waiting for transfers between devices: none -> 58.1 us  [the longest x1 22.8 us: partner_weight(): third = lax.ppermute(second, 'x', DOWN)]
    ppermute x0 -> x24, starting transfers between devices: none -> 28.2 us  [the longest x3 6.33 us: local(): sums[target] = (kept, lax.ppermute(given, 'zh', SWAP))]
    dynamic_update_slice x10 -> x0, other arithmetic: 16 us -> none  [local(): lax.dynamic_update_slice(grad_terms, current + block[None, None], corner)]
  transfers between devices with their start and end apart: 3 -> 31, of which waited for: 3 -> 11; matrix products, arithmetic and copies ran while one was open for 7% -> 6% of each run, Pallas kernels for 0% -> 37%
where the time goes in v1:
time: 308 us; the launch traced here: 306 us
  Pallas kernels  113 us (37%)
  local copies, waits for them, and re-layouts  83.6 us (27%)
  waiting for transfers between devices  59 us (19%)
  starting transfers between devices  28.7 us (9%)
  between operations  15 us (5%)
  other arithmetic  6.56 us (2%)
    unnamed x154, local copies, waits for them, and re-layouts  70.1 us
    pallas_call x4, Pallas kernels, backward(): pl.pallas_call(functools.partial(backward_kernel, level), grid_spec=pltpu...  42.1 us
    pallas_call x4, Pallas kernels, probs(): pl.pallas_call(functools.partial(probs_kernel, level), grid_spec=pltpu.Pr...  23.8 us
    ppermute x1, waiting for transfers between devices, partner_weight(): third = lax.ppermute(second, 'x', DOWN)  22.8 us
    pallas_call x4, Pallas kernels, own_product(): pl.pallas_call(own_product_kernel, grid_spec=pltpu.PrefetchScalarGridSpec...  21.8 us
    pallas_call x4, Pallas kernels, partner_product(): pl.pallas_call(partner_product_kernel, grid=(4,), in_specs=[pl.BlockSpec(...  20.7 us
    ppermute x1, waiting for transfers between devices, gather_rows(): pair = jnp.stack([own, lax.ppermute(own, 'zh', SWAP)])  9.02 us
    ppermute x1, waiting for transfers between devices, gather_rows(): above = lax.ppermute(pair, 'x', DOWN)  8.61 us
  transfers between devices with their start and end apart: 31, of which 11 were waited for; matrix products, arithmetic and copies ran while one was open for 6% of the time, Pallas kernels for 37%

profile of v1, /device:TPU:0, one launch (start us, length us, event | category | flops | bytes accessed | tf_op | source)
XLA Modules:
  0.0 305.8 jit_solution(3090989630340418384)
XLA Ops:
  7.2 2.9 fusion.8
  11.1 4.0 %collective-permute-start.9 = (bf16[3,2,256,128]{3,2,1,0:T(8,128)(2,1)S(1)}, bf16[3,2,256,128]{3,2,1,0:T(8,128)(2,1)S(1)}, u32[]{:S(2)}, u32[]{:S(2)}) collective-permute-start(bf16[3,2,256,128]{3,2,1,0:T(8,128)(2,1)S(1)} %get-tuple-element.50), channel_id=1, source_target_pairs={{0,64},{64,0},{1,65},{65,1},{2,66},{66,2},{3,67},{67,3},{4,68},{68... | collective-permute-start | bytes 1179656 | tf_op jit(solution)/shard_map/ppermute | solution.py:310
  15.3 9.0 %collective-permute-done.9 = bf16[3,2,256,128]{3,2,1,0:T(8,128)(2,1)S(1)} collective-permute-done((bf16[3,2,256,128]{3,2,1,0:T(8,128)(2,1)S(1)}, bf16[3,2,256,128]{3,2,1,0:T(8,128)(2,1)S(1)}, u32[]{:S(2)}, u32[]{:S(2)}) %collective-permute-start.9) | collective-permute-done | bytes 393248 | tf_op jit(solution)/shard_map/ppermute | solution.py:310
  24.4 2.8 collective-permute-start.10
  27.2 1.7 fusion.7
  30.2 2.5 collective-permute-start.1
  34.8 8.6 %collective-permute-done.10 = bf16[2,3,2,256,128]{4,3,2,1,0:T(8,128)(2,1)S(1)} collective-permute-done((bf16[2,3,2,256,128]{4,3,2,1,0:T(8,128)(2,1)S(1)}, bf16[2,3,2,256,128]{4,3,2,1,0:T(8,128)(2,1)S(1)}, u32[]{:S(2)}, u32[]{:S(2)}) %collective-permute-start.10) | collective-permute-done | bytes 786464 | tf_op jit(solution)/shard_map/ppermute | solution.py:312
  43.5 3.8 %collective-permute-start.11 = (bf16[3,2,256,128]{3,2,1,0:T(8,128)(2,1)S(1)}, bf16[3,2,256,128]{3,2,1,0:T(8,128)(2,1)S(1)}, u32[]{:S(2)}, u32[]{:S(2)}) collective-permute-start(bf16[3,2,256,128]{3,2,1,0:T(8,128)(2,1)S(1)} %slice_bitcast_fusion.1), channel_id=1, source_target_pairs={{0,48},{16,0},{32,16},{48,32},{1,49},{17,1},{33,17},{49,33},{2,50}... | collective-permute-start | bytes 1179656 | tf_op jit(solution)/shard_map/ppermute | solution.py:314
  47.3 1.5 constant_dynamic-update-slice_fusion.1
  48.8 5.4 %collective-permute-done.11 = bf16[3,2,256,128]{3,2,1,0:T(8,128)(2,1)S(1)} collective-permute-done((bf16[3,2,256,128]{3,2,1,0:T(8,128)(2,1)S(1)}, bf16[3,2,256,128]{3,2,1,0:T(8,128)(2,1)S(1)}, u32[]{:S(2)}, u32[]{:S(2)}) %collective-permute-start.11) | collective-permute-done | bytes 393248 | tf_op jit(solution)/shard_map/ppermute | solution.py:314
  55.2 2.5 collective-permute-done.13
  58.8 1.5 constant_dynamic-update-slice_fusion
  63.1 22.8 %collective-permute-done.2.refs_2_ = bf16[128,4096]{1,0:T(8,128)(2,1)S(1)} collective-permute-done((bf16[128,4096]{1,0:T(8,128)(2,1)S(1)}, bf16[128,4096]{1,0:T(8,128)(2,1)S(1)}, u32[]{:S(2)}, u32[]{:S(2)}) %collective-permute-start.2) | collective-permute-done | bytes 1048608 | tf_op jit(solution)/shard_map/ppermute | solution.py:328
  85.9 2.2 collective-permute-done.3.refs_3_
  97.0 1.6 copy-done.38
  98.6 5.5 %partner_product.7 = bf16[8,256,128]{2,1,0:T(8,128)(2,1)} custom-call(bf16[4,256,1024]{2,1,0:T(8,128)(2,1)S(1)} %bitcast.72, bf16[128,4096]{1,0:T(8,128)(2,1)S(1)} %collective-permute-done.refs_0_, bf16[128,4096]{1,0:T(8,128)(2,1)S(1)} %collective-permute-done.1.refs_1_, bf16[128,4096]{1,0:T(8,128)(2,1)S(1)} %collective-permute-done.2.refs_2_, ...), custom_call_target="tpu_custom_call" | custom-call | flops 2147483648 | bytes 9437184 | tf_op jit(solution)/shard_map/partner_product/pallas_call | solution.py:104
  105.1 5.8 %copy-done = bf16[1024,8192]{1,0:T(8,128)(2,1)S(1)} copy-done((bf16[1024,8192]{1,0:T(8,128)(2,1)S(1)}, bf16[1024,8192]{1,0:T(8,128)(2,1)}, u32[]{:S(2)}) %copy-start) | copy-done | bytes 16777240
  110.8 1.6 copy-done.39
  112.4 5.5 %own_product.7.own = f32[256,1024]{1,0:T(8,128)S(1)} custom-call(s32[5]{0:T(128)S(1)} %stack.78.meta, bf16[4,256,1024]{2,1,0:T(8,128)(2,1)S(1)} %bitcast.73, bf16[1024,8192]{1,0:T(8,128)(2,1)S(1)} %copy-done), custom_call_target="tpu_custom_call" | custom-call | flops 2147483648 | bytes 9961472 | tf_op jit(solution)/shard_map/own_product/pallas_call | solution.py:65
  117.9 4.2 %constant_dynamic-update-slice_fusion.4.refs_0_.refs_1_.refs_2_.refs_3_.refs_4_.refs_5_ = bf16[16,3,2,256,128]{4,3,2,1,0:T(8,128)(2,1)} fusion(bf16[16,3,2,256,128]{4,3,2,1,0:T(8,128)(2,1)} %get-tuple-element.38, bf16[8,3,2,256,128]{4,3,2,1,0:T(8,128)(2,1)} %collective-permute-done.14), kind=kLoop, calls=%fused_computation.35 | loop fusion | bytes 6291456 | tf_op jit(solution)/shard_map/concatenate | solution.py:317
  122.1 8.8 %probs_3.1.probs_ref = bf16[8,1024,256]{2,1,0:T(8,128)(2,1)S(1)} custom-call(s32[5]{0:T(128)S(1)} %stack.78.meta, s32[48]{0:T(128)S(1)} %reshape.159.parents, s32[64]{0:T(128)S(1)} %reshape.160.lengths, bf16[4,1,256,1024]{3,2,1,0:T(8,128)(2,1)S(1)} %copy-done.4, bf16[4,1,256,128]{3,2,1,0:T(8,128)(2,1)S(1)} %copy-done.5, ...), custom_call_target="tpu_custom_call" | custom-call | flops 536870912 | bytes 4194304 | tf_op jit(solution)/shard_map/probs_3/pallas_call | solution.py:149
  131.0 14.8 %backward_3.1 = (bf16[256,1024]{1,0:T(8,128)(2,1)S(1)}, f32[2,256,128]{2,1,0:T(8,128)S(1)}, bf16[3,2,256,128]{3,2,1,0:T(8,128)(2,1)S(1)}) custom-call(s32[5]{0:T(128)S(1)} %stack.78.meta, s32[48]{0:T(128)S(1)} %reshape.159.parents, s32[64]{0:T(128)S(1)} %reshape.160.lengths, bf16[8,1024,256]{2,1,0:T(8,128)(2,1)S(1)} %probs_3.1.probs_ref, ...), custom_call_target="tpu_custom_call" | custom-call | flops 2147483648 | bytes 4194304 | tf_op jit(solution)/shard_map/backward_3/pallas_call | solution.py:244
  146.0 1.6 collective-permute-done.20.refs_5_.refs_3_.refs_1_
  157.4 1.6 copy-done.36
  159.0 4.9 %partner_product.6 = bf16[8,256,128]{2,1,0:T(8,128)(2,1)S(1)} custom-call(bf16[4,256,1024]{2,1,0:T(8,128)(2,1)S(1)} %bitcast.70, bf16[128,4096]{1,0:T(8,128)(2,1)S(1)} %collective-permute-done.refs_0_, bf16[128,4096]{1,0:T(8,128)(2,1)S(1)} %copy-done.7, bf16[128,4096]{1,0:T(8,128)(2,1)S(1)} %copy-done.11, bf16[128,4096]{1,0:T(8,128)(2,1)} %collective-permute-done.3.refs_3_, ...), custom_call_target="tpu_custom_call" | custom-call | flops 2147483648 | bytes 9437184 | tf_op jit(solution)/shard_map/partner_product/pallas_call | solution.py:104
  165.2 5.9 %copy-done.1 = bf16[1024,8192]{1,0:T(8,128)(2,1)S(1)} copy-done((bf16[1024,8192]{1,0:T(8,128)(2,1)S(1)}, bf16[1024,8192]{1,0:T(8,128)(2,1)}, u32[]{:S(2)}) %copy-start.1) | copy-done | bytes 16777240
  171.1 5.5 %own_product.6.own = f32[256,1024]{1,0:T(8,128)S(1)} custom-call(s32[5]{0:T(128)S(1)} %stack.78.meta, bf16[4,256,1024]{2,1,0:T(8,128)(2,1)S(1)} %bitcast.71, bf16[1024,8192]{1,0:T(8,128)(2,1)S(1)} %copy-done.1), custom_call_target="tpu_custom_call" | custom-call | flops 2147483648 | bytes 9961472 | tf_op jit(solution)/shard_map/own_product/pallas_call | solution.py:65
  176.6 6.8 %probs_2.1.probs_ref = bf16[8,768,256]{2,1,0:T(8,128)(2,1)S(1)} custom-call(s32[5]{0:T(128)S(1)} %stack.78.meta, s32[48]{0:T(128)S(1)} %reshape.159.parents, s32[64]{0:T(128)S(1)} %reshape.160.lengths, bf16[4,1,256,1024]{3,2,1,0:T(8,128)(2,1)S(1)} %copy-done.4, bf16[4,1,256,128]{3,2,1,0:T(8,128)(2,1)S(1)} %copy-done.5, ...), custom_call_target="tpu_custom_call" | custom-call | flops 402653184 | bytes 3145728 | tf_op jit(solution)/shard_map/probs_2/pallas_call | solution.py:149
  183.4 12.2 %backward_2.1 = (bf16[256,1024]{1,0:T(8,128)(2,1)S(1)}, f32[2,256,128]{2,1,0:T(8,128)S(1)}, bf16[2,2,256,128]{3,2,1,0:T(8,128)(2,1)S(1)}) custom-call(s32[5]{0:T(128)S(1)} %stack.78.meta, s32[48]{0:T(128)S(1)} %reshape.159.parents, s32[64]{0:T(128)S(1)} %reshape.160.lengths, bf16[8,768,256]{2,1,0:T(8,128)(2,1)S(1)} %probs_2.1.probs_ref, ...), custom_call_target="tpu_custom_call" | custom-call | flops 1610612736 | bytes 3145728 | tf_op jit(solution)/shard_map/backward_2/pallas_call | solution.py:244
  195.7 1.5 collective-permute-done.19.refs_4_.refs_2_
  197.2 1.5 spread_1.1
  207.2 1.8 copy-done.34
  209.0 4.9 %partner_product.5 = bf16[8,256,128]{2,1,0:T(8,128)(2,1)S(1)} custom-call(bf16[4,256,1024]{2,1,0:T(8,128)(2,1)S(1)} %bitcast.68, bf16[128,4096]{1,0:T(8,128)(2,1)S(1)} %collective-permute-done.refs_0_, bf16[128,4096]{1,0:T(8,128)(2,1)S(1)} %copy-done.8, bf16[128,4096]{1,0:T(8,128)(2,1)S(1)} %copy-done.12, bf16[128,4096]{1,0:T(8,128)(2,1)} %collective-permute-done.3.refs_3_, ...), custom_call_target="tpu_custom_call" | custom-call | flops 2147483648 | bytes 9437184 | tf_op jit(solution)/shard_map/partner_product/pallas_call | solution.py:104
  214.6 5.9 %copy-done.2 = bf16[1024,8192]{1,0:T(8,128)(2,1)S(1)} copy-done((bf16[1024,8192]{1,0:T(8,128)(2,1)S(1)}, bf16[1024,8192]{1,0:T(8,128)(2,1)}, u32[]{:S(2)}) %copy-start.2) | copy-done | bytes 16777240
  220.5 5.5 %own_product.5.own = f32[256,1024]{1,0:T(8,128)S(1)} custom-call(s32[5]{0:T(128)S(1)} %stack.78.meta, bf16[4,256,1024]{2,1,0:T(8,128)(2,1)S(1)} %bitcast.69, bf16[1024,8192]{1,0:T(8,128)(2,1)S(1)} %copy-done.2), custom_call_target="tpu_custom_call" | custom-call | flops 2147483648 | bytes 9961472 | tf_op jit(solution)/shard_map/own_product/pallas_call | solution.py:65
  225.9 5.2 %probs_1.1.probs_ref = bf16[8,512,256]{2,1,0:T(8,128)(2,1)S(1)} custom-call(s32[5]{0:T(128)S(1)} %stack.78.meta, s32[48]{0:T(128)S(1)} %reshape.159.parents, s32[64]{0:T(128)S(1)} %reshape.160.lengths, bf16[4,1,256,1024]{3,2,1,0:T(8,128)(2,1)S(1)} %copy-done.4, bf16[4,1,256,128]{3,2,1,0:T(8,128)(2,1)S(1)} %copy-done.5, ...), custom_call_target="tpu_custom_call" | custom-call | flops 268435456 | bytes 2097152 | tf_op jit(solution)/shard_map/probs_1/pallas_call | solution.py:149
  231.2 9.5 %backward_1.1 = (bf16[256,1024]{1,0:T(8,128)(2,1)S(1)}, f32[2,256,128]{2,1,0:T(8,128)S(1)}, bf16[1,2,256,128]{3,2,1,0:T(8,128)(2,1)S(1)}) custom-call(s32[5]{0:T(128)S(1)} %stack.78.meta, s32[48]{0:T(128)S(1)} %reshape.159.parents, s32[64]{0:T(128)S(1)} %reshape.160.lengths, bf16[8,512,256]{2,1,0:T(8,128)(2,1)S(1)} %probs_1.1.probs_ref, ...), custom_call_target="tpu_custom_call" | custom-call | flops 1073741824 | bytes 2097152 | tf_op jit(solution)/shard_map/backward_1/pallas_call | solution.py:244
  242.2 1.9 spread_0.1
  252.6 1.6 copy-done.40
  254.2 5.5 %partner_product.4 = bf16[8,256,128]{2,1,0:T(8,128)(2,1)} custom-call(bf16[4,256,1024]{2,1,0:T(8,128)(2,1)S(1)} %bitcast.74, bf16[128,4096]{1,0:T(8,128)(2,1)S(1)} %collective-permute-done.refs_0_, bf16[128,4096]{1,0:T(8,128)(2,1)S(1)} %copy-done.9, bf16[128,4096]{1,0:T(8,128)(2,1)S(1)} %copy-done.13, bf16[128,4096]{1,0:T(8,128)(2,1)} %collective-permute-done.3.refs_3_, ...), custom_call_target="tpu_custom_call" | custom-call | flops 2147483648 | bytes 9437184 | tf_op jit(solution)/shard_map/partner_product/pallas_call | solution.py:104
  261.1 3.0 probs_0.1.probs_ref
  264.1 5.9 %copy-done.3 = bf16[1024,8192]{1,0:T(8,128)(2,1)S(1)} copy-done((bf16[1024,8192]{1,0:T(8,128)(2,1)S(1)}, bf16[1024,8192]{1,0:T(8,128)(2,1)}, u32[]{:S(2)}) %copy-start.3) | copy-done | bytes 16777240
  270.0 5.5 %own_product.4.own = f32[256,1024]{1,0:T(8,128)S(1)} custom-call(s32[5]{0:T(128)S(1)} %stack.78.meta, bf16[4,256,1024]{2,1,0:T(8,128)(2,1)S(1)} %bitcast.75, bf16[1024,8192]{1,0:T(8,128)(2,1)S(1)} %copy-done.3), custom_call_target="tpu_custom_call" | custom-call | flops 2147483648 | bytes 9961472 | tf_op jit(solution)/shard_map/own_product/pallas_call | solution.py:65
  275.5 5.6 %backward_0.1 = (bf16[256,1024]{1,0:T(8,128)(2,1)S(1)}, f32[2,256,128]{2,1,0:T(8,128)S(1)}) custom-call(s32[5]{0:T(128)S(1)} %stack.78.meta, s32[48]{0:T(128)S(1)} %reshape.159.parents, s32[64]{0:T(128)S(1)} %reshape.160.lengths, bf16[8,256,256]{2,1,0:T(8,128)(2,1)S(1)} %probs_0.1.probs_ref, bf16[4,1,256,1024]{3,2,1,0:T(8,128)(2,1)S(1)} %copy-done.4, ...), custom_call_target="tpu_custom_call" | custom-call | flops 536870912 | bytes 1048576 | tf_op jit(solution)/shard_map/backward_0/pallas_call | solution.py:244
  281.3 1.6 maximum_bitcast_fusion
  283.8 2.6 collective-permute-start.23
  289.3 2.6 collective-permute-start.21
  293.0 2.4 collective-permute-done.22
  (221 shorter events, 59.5 us)
Async XLA Ops:
  7.2 84.9 %all-gather.15.cloned.1.call-start = ((), (), s32[]{:S(2)}) async-start(), calls=%async_computation.9 | async-start | bytes 2621440 | tf_op jit(solution)/shard_map/all_gather | solution.py:341
  10.2 139.8 %all-gather.13.cloned.1.call-start = ((), (), s32[]{:S(2)}) async-start(), calls=%async_computation.8 | async-start | bytes 2621440 | tf_op jit(solution)/shard_map/all_gather | solution.py:341
  10.9 188.9 %all-gather.11.cloned.1.call-start = ((), (), s32[]{:S(2)}) async-start(), calls=%async_computation.7 | async-start | bytes 2621440 | tf_op jit(solution)/shard_map/all_gather | solution.py:341
  11.1 13.2 %collective-permute-start.9 = (bf16[3,2,256,128]{3,2,1,0:T(8,128)(2,1)S(1)}, bf16[3,2,256,128]{3,2,1,0:T(8,128)(2,1)S(1)}, u32[]{:S(2)}, u32[]{:S(2)}) collective-permute-start(bf16[3,2,256,128]{3,2,1,0:T(8,128)(2,1)S(1)} %get-tuple-element.50), channel_id=1, source_target_pairs={{0,64},{64,0},{1,65},{65,1},{2,66},{66,2},{3,67},{67,3},{4,68},{68... | collective-permute-start | bytes 1179656 | tf_op jit(solution)/shard_map/ppermute | solution.py:310
  15.2 230.0 %all-gather.9.cloned.1.call-start = ((), (), s32[]{:S(2)}) async-start(), calls=%async_computation.6 | async-start | bytes 2621440 | tf_op jit(solution)/shard_map/all_gather | solution.py:341
  24.4 19.1 %collective-permute-start.10 = (bf16[2,3,2,256,128]{4,3,2,1,0:T(8,128)(2,1)S(1)}, bf16[2,3,2,256,128]{4,3,2,1,0:T(8,128)(2,1)S(1)}, u32[]{:S(2)}, u32[]{:S(2)}) collective-permute-start(bf16[2,3,2,256,128]{4,3,2,1,0:T(8,128)(2,1)S(1)} %pad_maximum_fusion), channel_id=1, source_target_pairs={{0,48},{16,0},{32,16},{48,32},{1,49},{17,1},{33,17},{49,33},{2,50}... | collective-permute-start | bytes 2359304 | tf_op jit(solution)/shard_map/ppermute | solution.py:312
  27.2 20.0 %collective-permute-start.12 = (bf16[2,3,2,256,128]{4,3,2,1,0:T(8,128)(2,1)S(1)}, bf16[2,3,2,256,128]{4,3,2,1,0:T(8,128)(2,1)S(1)}, u32[]{:S(2)}, u32[]{:S(2)}) collective-permute-start(bf16[2,3,2,256,128]{4,3,2,1,0:T(8,128)(2,1)S(1)} %pad_maximum_fusion), channel_id=1, source_target_pairs={{0,16},{16,32},{32,48},{48,0},{1,17},{17,33},{33,49},{49,1},{2,18}... | collective-permute-start | bytes 2359304 | tf_op jit(solution)/shard_map/ppermute | solution.py:311
  28.9 32.7 %collective-permute-start = (bf16[128,4096]{1,0:T(8,128)(2,1)S(1)}, bf16[128,4096]{1,0:T(8,128)(2,1)S(1)}, u32[]{:S(2)}, u32[]{:S(2)}) collective-permute-start(bf16[128,4096]{1,0:T(8,128)(2,1)S(1)} %get-tuple-element.32), channel_id=1, source_target_pairs={{0,4},{4,0},{1,5},{5,1},{2,6},{6,2},{3,7},{7,3},{8,12},{12,8},{9,1... | collective-permute-start | bytes 3145736 | tf_op jit(solution)/shard_map/ppermute | solution.py:326
  30.2 30.1 %collective-permute-start.1 = (bf16[128,4096]{1,0:T(8,128)(2,1)S(1)}, bf16[128,4096]{1,0:T(8,128)(2,1)S(1)}, u32[]{:S(2)}, u32[]{:S(2)}) collective-permute-start(bf16[128,4096]{1,0:T(8,128)(2,1)S(1)} %get-tuple-element.31), channel_id=1, source_target_pairs={{0,68},{4,64},{64,4},{68,0},{1,69},{5,65},{65,5},{69,1},{2,70},{6,... | collective-permute-start | bytes 3145736 | tf_op jit(solution)/shard_map/ppermute | solution.py:327
  43.5 10.8 %collective-permute-start.11 = (bf16[3,2,256,128]{3,2,1,0:T(8,128)(2,1)S(1)}, bf16[3,2,256,128]{3,2,1,0:T(8,128)(2,1)S(1)}, u32[]{:S(2)}, u32[]{:S(2)}) collective-permute-start(bf16[3,2,256,128]{3,2,1,0:T(8,128)(2,1)S(1)} %slice_bitcast_fusion.1), channel_id=1, source_target_pairs={{0,48},{16,0},{32,16},{48,32},{1,49},{17,1},{33,17},{49,33},{2,50}... | collective-permute-start | bytes 1179656 | tf_op jit(solution)/shard_map/ppermute | solution.py:314
  47.3 10.5 %collective-permute-start.13 = (bf16[3,2,256,128]{3,2,1,0:T(8,128)(2,1)S(1)}, bf16[3,2,256,128]{3,2,1,0:T(8,128)(2,1)S(1)}, u32[]{:S(2)}, u32[]{:S(2)}) collective-permute-start(bf16[3,2,256,128]{3,2,1,0:T(8,128)(2,1)S(1)} %slice_bitcast_fusion), channel_id=1, source_target_pairs={{0,16},{16,32},{32,48},{48,0},{1,17},{17,33},{33,49},{49,1},{2,18}... | collective-permute-start | bytes 1179656 | tf_op jit(solution)/shard_map/ppermute | solution.py:314
  60.3 57.6 %collective-permute-start.14 = (bf16[8,3,2,256,128]{4,3,2,1,0:T(8,128)(2,1)}, bf16[8,3,2,256,128]{4,3,2,1,0:T(8,128)(2,1)}, u32[]{:S(2)}, u32[]{:S(2)}) collective-permute-start(bf16[8,3,2,256,128]{4,3,2,1,0:T(8,128)(2,1)} %get-tuple-element.37), channel_id=1, source_target_pairs={{0,8},{8,0},{1,9},{9,1},{2,10},{10,2},{3,11},{11,3},{4,12},{12,4},... | collective-permute-start | bytes 9437192 | tf_op jit(solution)/shard_map/ppermute | solution.py:317
  60.3 43.8 %copy-start.6 = (bf16[128,4096]{1,0:T(8,128)(2,1)}, bf16[128,4096]{1,0:T(8,128)(2,1)S(1)}, u32[]{:S(2)}) copy-start(bf16[128,4096]{1,0:T(8,128)(2,1)S(1)} %collective-permute-done.1.refs_1_) | copy-start | bytes 3145732
  60.3 25.6 %collective-permute-start.2 = (bf16[128,4096]{1,0:T(8,128)(2,1)S(1)}, bf16[128,4096]{1,0:T(8,128)(2,1)S(1)}, u32[]{:S(2)}, u32[]{:S(2)}) collective-permute-start(bf16[128,4096]{1,0:T(8,128)(2,1)S(1)} %collective-permute-done.1.refs_1_), channel_id=1, source_target_pairs={{0,48},{16,0},{32,16},{48,32},{1,49},{17,1},{33,17},{49,33},{2,50}... | collective-permute-start | bytes 3145736 | tf_op jit(solution)/shard_map/ppermute | solution.py:328
  61.6 26.5 %collective-permute-start.3 = (bf16[128,4096]{1,0:T(8,128)(2,1)S(1)}, bf16[128,4096]{1,0:T(8,128)(2,1)}, u32[]{:S(2)}, u32[]{:S(2)}) collective-permute-start(bf16[128,4096]{1,0:T(8,128)(2,1)S(1)} %collective-permute-done.refs_0_), channel_id=1, source_target_pairs={{0,16},{16,32},{32,48},{48,0},{1,17},{17,33},{33,49},{49,1},{2,18}... | collective-permute-start | bytes 3145736 | tf_op jit(solution)/shard_map/ppermute | solution.py:329
  62.4 220.5 %reduce-scatter.8.cloned.1.call-start = ((), (), s32[]{:S(2)}) async-start(), calls=%async_computation.5 | async-start | bytes 1310720 | tf_op jit(solution)/shard_map/reduce_scatter | solution.py:363
  62.5 25.6 %collective-permute-start.4 = (bf16[128,4096]{1,0:T(8,128)(2,1)S(1)}, bf16[128,4096]{1,0:T(8,128)(2,1)S(1)}, u32[]{:S(2)}, u32[]{:S(2)}) collective-permute-start(bf16[128,4096]{1,0:T(8,128)(2,1)S(1)} %collective-permute-done.refs_0_), channel_id=1, source_target_pairs={{0,8},{8,0},{1,9},{9,1},{2,10},{10,2},{3,11},{11,3},{4,12},{12,4},... | collective-permute-start | bytes 3145736 | tf_op jit(solution)/shard_map/ppermute | solution.py:331
  62.6 26.5 %collective-permute-start.5 = (bf16[128,4096]{1,0:T(8,128)(2,1)S(1)}, bf16[128,4096]{1,0:T(8,128)(2,1)S(1)}, u32[]{:S(2)}, u32[]{:S(2)}) collective-permute-start(bf16[128,4096]{1,0:T(8,128)(2,1)S(1)} %collective-permute-done.1.refs_1_), channel_id=1, source_target_pairs={{0,8},{8,0},{1,9},{9,1},{2,10},{10,2},{3,11},{11,3},{4,12},{12,4},... | collective-permute-start | bytes 3145736 | tf_op jit(solution)/shard_map/ppermute | solution.py:331
  85.9 18.2 %copy-start.10 = (bf16[128,4096]{1,0:T(8,128)(2,1)}, bf16[128,4096]{1,0:T(8,128)(2,1)S(1)}, u32[]{:S(2)}) copy-start(bf16[128,4096]{1,0:T(8,128)(2,1)S(1)} %collective-permute-done.2.refs_2_) | copy-start | bytes 3145732
  85.9 4.3 %collective-permute-start.6 = (bf16[128,4096]{1,0:T(8,128)(2,1)S(1)}, bf16[128,4096]{1,0:T(8,128)(2,1)S(1)}, u32[]{:S(2)}, u32[]{:S(2)}) collective-permute-start(bf16[128,4096]{1,0:T(8,128)(2,1)S(1)} %collective-permute-done.2.refs_2_), channel_id=1, source_target_pairs={{0,8},{8,0},{1,9},{9,1},{2,10},{10,2},{3,11},{11,3},{4,12},{12,4},... | collective-permute-start | bytes 3145736 | tf_op jit(solution)/shard_map/ppermute | solution.py:331
  88.1 3.0 collective-permute-start.7
  98.6 6.2 %copy-start.73 = (s32[3,16]{1,0:T(4,128)S(1)}, s32[3,16]{1,0:T(4,128)}, u32[]{:S(2)}) copy-start(s32[3,16]{1,0:T(4,128)} %param.12) | copy-start | bytes 580
  98.6 6.3 %copy-start.74 = (s32[4,16]{1,0:T(4,128)S(1)}, s32[4,16]{1,0:T(4,128)}, u32[]{:S(2)}) copy-start(s32[4,16]{1,0:T(4,128)} %param.13) | copy-start | bytes 772
  104.1 26.9 %collective-permute-start.17 = (bf16[8,256,128]{2,1,0:T(8,128)(2,1)}, bf16[8,256,128]{2,1,0:T(8,128)(2,1)}, u32[]{:S(2)}, u32[]{:S(2)}) collective-permute-start(bf16[8,256,128]{2,1,0:T(8,128)(2,1)} %partner_product.7), channel_id=1, source_target_pairs={{0,4},{4,0},{1,5},{5,1},{2,6},{6,2},{3,7},{7,3},{8,12},{12,8},{9,1... | collective-permute-start | bytes 1572872 | tf_op jit(solution)/shard_map/ppermute | solution.py:350
  122.1 8.8 %copy-start.43 = (bf16[4,1,256,128]{3,2,1,0:T(8,128)(2,1)S(1)}, bf16[4,1,256,128]{3,2,1,0:T(8,128)(2,1)}, u32[]{:S(2)}) copy-start(bf16[4,1,256,128]{3,2,1,0:T(8,128)(2,1)} %own_value.7) | copy-start | bytes 786436
  145.8 1.8 collective-permute-start.20
  149.8 136.7 %reduce-scatter.6.cloned.1.call-start = ((), (), s32[]{:S(2)}) async-start(), calls=%async_computation.4 | async-start | bytes 1310720 | tf_op jit(solution)/shard_map/reduce_scatter | solution.py:363
  159.0 6.2 %copy-start.37 = (bf16[4,1,256,1024]{3,2,1,0:T(8,128)(2,1)S(1)}, bf16[4,1,256,1024]{3,2,1,0:T(8,128)(2,1)}, u32[]{:S(2)}) copy-start(bf16[4,1,256,1024]{3,2,1,0:T(8,128)(2,1)} %all-gather.13.cloned.1.call-done) | copy-start | bytes 6291460
  163.9 19.5 %collective-permute-start.16 = (bf16[8,256,128]{2,1,0:T(8,128)(2,1)S(1)}, bf16[8,256,128]{2,1,0:T(8,128)(2,1)S(1)}, u32[]{:S(2)}, u32[]{:S(2)}) collective-permute-start(bf16[8,256,128]{2,1,0:T(8,128)(2,1)S(1)} %partner_product.6), channel_id=1, source_target_pairs={{0,4},{4,0},{1,5},{5,1},{2,6},{6,2},{3,7},{7,3},{8,12},{12,8},{9,1... | collective-permute-start | bytes 1572872 | tf_op jit(solution)/shard_map/ppermute | solution.py:350
  165.2 5.9 %copy-start.1 = (bf16[1024,8192]{1,0:T(8,128)(2,1)S(1)}, bf16[1024,8192]{1,0:T(8,128)(2,1)}, u32[]{:S(2)}) copy-start(bf16[1024,8192]{1,0:T(8,128)(2,1)} %weight.7) | copy-start | bytes 50331652
  176.6 6.8 %copy-start.44 = (bf16[4,1,256,128]{3,2,1,0:T(8,128)(2,1)S(1)}, bf16[4,1,256,128]{3,2,1,0:T(8,128)(2,1)}, u32[]{:S(2)}) copy-start(bf16[4,1,256,128]{3,2,1,0:T(8,128)(2,1)} %own_value.7) | copy-start | bytes 786436
  183.3 13.9 %copy-start.51 = (bf16[3,2,256,128]{3,2,1,0:T(8,128)(2,1)S(1)}, bf16[3,2,256,128]{3,2,1,0:T(8,128)(2,1)}, u32[]{:S(2)}) copy-start(bf16[3,2,256,128]{3,2,1,0:T(8,128)(2,1)} %copy-done.50) | copy-start | bytes 1179652
  183.4 13.8 %copy-start.54 = (bf16[3,2,256,128]{3,2,1,0:T(8,128)(2,1)S(1)}, bf16[3,2,256,128]{3,2,1,0:T(8,128)(2,1)}, u32[]{:S(2)}) copy-start(bf16[3,2,256,128]{3,2,1,0:T(8,128)(2,1)} %copy-done.53) | copy-start | bytes 1179652
  195.6 1.6 collective-permute-start.19
  199.8 88.6 %reduce-scatter.4.cloned.1.call-start = ((), (), s32[]{:S(2)}) async-start(), calls=%async_computation.3 | async-start | bytes 1310720 | tf_op jit(solution)/shard_map/reduce_scatter | solution.py:363
  213.9 17.3 %collective-permute-start.15 = (bf16[8,256,128]{2,1,0:T(8,128)(2,1)S(1)}, bf16[8,256,128]{2,1,0:T(8,128)(2,1)S(1)}, u32[]{:S(2)}, u32[]{:S(2)}) collective-permute-start(bf16[8,256,128]{2,1,0:T(8,128)(2,1)S(1)} %partner_product.5), channel_id=1, source_target_pairs={{0,4},{4,0},{1,5},{5,1},{2,6},{6,2},{3,7},{7,3},{8,12},{12,8},{9,1... | collective-permute-start | bytes 1572872 | tf_op jit(solution)/shard_map/ppermute | solution.py:350
  231.2 11.0 %copy-start.52 = (bf16[3,2,256,128]{3,2,1,0:T(8,128)(2,1)S(1)}, bf16[3,2,256,128]{3,2,1,0:T(8,128)(2,1)}, u32[]{:S(2)}) copy-start(bf16[3,2,256,128]{3,2,1,0:T(8,128)(2,1)} %copy-done.50) | copy-start | bytes 1179652
  231.2 11.0 %copy-start.55 = (bf16[3,2,256,128]{3,2,1,0:T(8,128)(2,1)S(1)}, bf16[3,2,256,128]{3,2,1,0:T(8,128)(2,1)}, u32[]{:S(2)}) copy-start(bf16[3,2,256,128]{3,2,1,0:T(8,128)(2,1)} %copy-done.53) | copy-start | bytes 1179652
  231.2 11.0 %copy-start.57 = (bf16[2,2,256,128]{3,2,1,0:T(8,128)(2,1)S(1)}, bf16[2,2,256,128]{3,2,1,0:T(8,128)(2,1)}, u32[]{:S(2)}) copy-start(bf16[2,2,256,128]{3,2,1,0:T(8,128)(2,1)} %copy-done.56) | copy-start | bytes 786436
  231.2 11.0 %copy-start.59 = (bf16[2,2,256,128]{3,2,1,0:T(8,128)(2,1)S(1)}, bf16[2,2,256,128]{3,2,1,0:T(8,128)(2,1)}, u32[]{:S(2)}) copy-start(bf16[2,2,256,128]{3,2,1,0:T(8,128)(2,1)} %copy-done.58) | copy-start | bytes 786436
  240.8 1.4 collective-permute-start.18
  259.7 15.9 %collective-permute-start.8 = (bf16[8,256,128]{2,1,0:T(8,128)(2,1)}, bf16[8,256,128]{2,1,0:T(8,128)(2,1)S(1)}, u32[]{:S(2)}, u32[]{:S(2)}) collective-permute-start(bf16[8,256,128]{2,1,0:T(8,128)(2,1)} %partner_product.4), channel_id=1, source_target_pairs={{0,4},{4,0},{1,5},{5,1},{2,6},{6,2},{3,7},{7,3},{8,12},{12,8},{9,1... | collective-permute-start | bytes 1572872 | tf_op jit(solution)/shard_map/ppermute | solution.py:350
  264.1 5.9 %copy-start.3 = (bf16[1024,8192]{1,0:T(8,128)(2,1)S(1)}, bf16[1024,8192]{1,0:T(8,128)(2,1)}, u32[]{:S(2)}) copy-start(bf16[1024,8192]{1,0:T(8,128)(2,1)} %weight.7) | copy-start | bytes 50331652
  281.2 10.8 %copy-start.69 = (f32[2,256,128]{2,1,0:T(8,128)S(1)}, f32[2,256,128]{2,1,0:T(8,128)}, u32[]{:S(2)}) copy-start(f32[2,256,128]{2,1,0:T(8,128)} %copy-done.68) | copy-start | bytes 786436
  281.2 14.1 %copy-start.71 = (f32[2,256,128]{2,1,0:T(8,128)S(1)}, f32[2,256,128]{2,1,0:T(8,128)}, u32[]{:S(2)}) copy-start(f32[2,256,128]{2,1,0:T(8,128)} %copy-done.70) | copy-start | bytes 786436
  283.8 8.2 %collective-permute-start.23 = (bf16[2,256,128]{2,1,0:T(8,128)(2,1)S(1)}, bf16[2,256,128]{2,1,0:T(8,128)(2,1)S(1)}, u32[]{:S(2)}, u32[]{:S(2)}) collective-permute-start(bf16[2,256,128]{2,1,0:T(8,128)(2,1)S(1)} %dynamic-slice_bitcast_fusion), channel_id=1, source_target_pairs={{0,64},{64,0},{1,65},{65,1},{2,66},{66,2},{3,67},{67,3},{4,68},{68... | collective-permute-start | bytes 393224 | tf_op jit(solution)/shard_map/ppermute | solution.py:368
  287.4 8.0 %collective-permute-start.22 = (bf16[2,256,128]{2,1,0:T(8,128)(2,1)S(1)}, bf16[2,256,128]{2,1,0:T(8,128)(2,1)S(1)}, u32[]{:S(2)}, u32[]{:S(2)}) collective-permute-start(bf16[2,256,128]{2,1,0:T(8,128)(2,1)S(1)} %dynamic-slice_bitcast_fusion.1), channel_id=1, source_target_pairs={{0,64},{64,0},{1,65},{65,1},{2,66},{66,2},{3,67},{67,3},{4,68},{68... | collective-permute-start | bytes 393224 | tf_op jit(solution)/shard_map/ppermute | solution.py:368
  289.3 7.7 %collective-permute-start.21 = (bf16[2,256,128]{2,1,0:T(8,128)(2,1)S(1)}, bf16[2,256,128]{2,1,0:T(8,128)(2,1)S(1)}, u32[]{:S(2)}, u32[]{:S(2)}) collective-permute-start(bf16[2,256,128]{2,1,0:T(8,128)(2,1)S(1)} %dynamic-slice_bitcast_fusion.2), channel_id=1, source_target_pairs={{0,64},{64,0},{1,65},{65,1},{2,66},{66,2},{3,67},{67,3},{4,68},{68... | collective-permute-start | bytes 393224 | tf_op jit(solution)/shard_map/ppermute | solution.py:368
  (58 other events, 137.7 us)
Sparse Core Ops, SparseCore 0:
  10.3 33.3 all-gather.14
  45.3 30.8 all-gather.12
  77.9 30.8 all-gather.10
  110.3 30.8 all-gather.8
  149.9 23.7 reduce-scatter.7
  199.9 22.9 reduce-scatter.5
  245.3 23.6 reduce-scatter.3
